TPU v7x, 512 devices: a whole 4x8x8 slice. The times are simulated.
512 devices in a mesh: row: 32 (over y, z_hi), col: 16 (over x, z_lo, core).
Axes of the slice: x: 4, y: 8, z: 8 (z_hi: 4, z_lo: 2; z = z_hi * 2 + z_lo), core: 2. Of those that a mesh axis runs over, the one named last changes fastest.
Arguments:
- features: bfloat16 [65536, 128], P(('row', 'col')), may hold values from -6 to 6
- adj_tiles: bfloat16 [49152, 128, 128], P(('row', 'col')), may hold values from -1 to 1
- tile_dest: int32 [49152], P(('row', 'col')), may hold values from 0 to 15
- tile_src: int32 [49152], P(('row', 'col')), may hold values from 0 to 31
- live_tiles: int32 [512], P(('row', 'col')), may hold values from 1 to 96, as said below
- degrees: int32 [65536], P(('row', 'col')), may hold values from 8 to 64
- self_one: bfloat16 [128, 256], replicated, may hold values from -0.5 to 0.5
- neigh_one: bfloat16 [128, 256], replicated, may hold values from -0.5 to 0.5
- bias_one: float32 [256], replicated, may hold values from -3 to 3
- self_two: bfloat16 [256, 256], replicated, may hold values from -0.375 to 0.375
- neigh_two: bfloat16 [256, 256], replicated, may hold values from -0.375 to 0.375
- bias_two: float32 [256], replicated, may hold values from -3 to 3
Outputs:
- embeddings: bfloat16 [65536, 256], P(('row', 'col'))
Inputs may be any that keep to these rules, and one draw needn't show every extreme that they name: `live_tiles`: slots at or above a device's count are not part of the adjacency. Some device has all 96 slots live.
All inputs are finite; a program needn't handle non-finite values.
Results may differ from a plain program's by a relative error of at most 0.018.
Values may be sent and summed in bfloat16 or wider, within the bound.
A program may use at most 64 MiB of HBM per device.

v0:
```python
import math

import jax
import jax.numpy as jnp
from jax import lax
from jax.sharding import PartitionSpec as P


def normalize_relu(pre_values):
    positive = jnp.maximum(pre_values, 0.0)
    mean_square = jnp.mean(positive * positive, axis=-1, keepdims=True)
    return (positive * lax.rsqrt(mean_square + 1e-05)).astype(jnp.bfloat16)


def accumulate(source_rows, adj_tiles, tile_dest, tile_src, live_count, dest_count, float_sources):
    feat_width = source_rows.shape[1]
    source_tiles = source_rows.reshape(source_rows.shape[0] // 128, 128, feat_width)
    slot_count = adj_tiles.shape[0]
    group_size = math.gcd(slot_count, 32)
    group_total = slot_count // group_size
    positions = jnp.arange(dest_count, dtype=jnp.int32)
    lane_index = jnp.arange(group_size, dtype=jnp.int32)

    def add_group(group_index, running):
        offset = group_index * group_size
        tile_block = lax.dynamic_slice_in_dim(adj_tiles, offset, group_size, 0)
        dest_block = lax.dynamic_slice_in_dim(tile_dest, offset, group_size, 0)
        src_block = lax.dynamic_slice_in_dim(tile_src, offset, group_size, 0)
        picked = jnp.take(source_tiles, src_block, axis=0)
        if float_sources:
            products = jnp.einsum(
                "gij,gjw->giw",
                tile_block.astype(jnp.float32),
                picked,
                precision=lax.Precision.HIGHEST,
            )
        else:
            products = jnp.einsum(
                "gij,gjw->giw", tile_block, picked, preferred_element_type=jnp.float32
            )
        is_live = offset + lane_index < live_count
        onehot = jnp.where(
            is_live[:, None] & (dest_block[:, None] == positions[None, :]), 1.0, 0.0
        ).astype(jnp.float32)
        return running + jnp.einsum(
            "gn,giw->niw", onehot, products, precision=lax.Precision.HIGHEST
        )

    initial = jnp.zeros((dest_count, 128, feat_width), jnp.float32)
    running = lax.fori_loop(0, group_total, add_group, initial)
    return running.reshape(dest_count * 128, feat_width)


def shards(
    features,
    adj_tiles,
    tile_dest,
    tile_src,
    live_tiles,
    degrees,
    self_one,
    neigh_one,
    bias_one,
    self_two,
    neigh_two,
    bias_two,
):
    divisor = degrees.astype(jnp.float32)[:, None]
    live_count = live_tiles[0]
    dest_count = lax.axis_size("col") * (features.shape[0] // 128)
    projected = jnp.dot(features, neigh_one, preferred_element_type=jnp.float32)
    column_rows = lax.all_gather(projected.astype(jnp.bfloat16), "row", axis=0, tiled=True).astype(
        projected.dtype
    )
    partial_value = accumulate(
        column_rows, adj_tiles, tile_dest, tile_src, live_count, dest_count, True
    )
    neighbour = (
        lax.psum_scatter(
            partial_value.astype(jnp.bfloat16), "col", scatter_dimension=0, tiled=True
        ).astype(jnp.float32)
        / divisor
    )
    pre_one = jnp.dot(features, self_one, preferred_element_type=jnp.float32) + neighbour + bias_one
    hidden = normalize_relu(pre_one)
    hidden_rows = lax.all_gather(hidden, "row", axis=0, tiled=True)
    partial_two = accumulate(
        hidden_rows, adj_tiles, tile_dest, tile_src, live_count, dest_count, False
    )
    second = (
        lax.psum_scatter(
            partial_two.astype(jnp.bfloat16), "col", scatter_dimension=0, tiled=True
        ).astype(jnp.float32)
        / divisor
    )
    pre_two = jnp.dot(hidden, self_two, preferred_element_type=jnp.float32)
    pre_two = pre_two + jnp.dot(
        second, neigh_two.astype(jnp.float32), precision=lax.Precision.HIGHEST
    )
    pre_two = pre_two + bias_two
    return normalize_relu(pre_two)


def solution(mesh):
    in_specs = (
        P(("row", "col"), None),
        P(("row", "col"), None, None),
        P(("row", "col")),
        P(("row", "col")),
        P(("row", "col")),
        P(("row", "col")),
        P(),
        P(),
        P(),
        P(),
        P(),
        P(),
    )
    out_specs = P(("row", "col"), None)
    return jax.shard_map(shards, mesh=mesh, in_specs=in_specs, out_specs=out_specs, check_vma=False)
```

profile of v0, /device:TPU:1, one launch (start us, length us, event | category | flops | bytes accessed | tf_op | source)
XLA Modules:
  0.0 438.9 jit_solution(7960608251404125697)
XLA Ops:
  6.5 1.7 convolution_convert_fusion
  8.3 91.8 %all-gather.3.cloned.1.call-done = bf16[4096,256]{1,0:T(8,128)(2,1)} async-done(((bf16[128,256]{1,0:T(8,128)(2,1)}), bf16[4096,256]{1,0:T(8,128)(2,1)}) %all-gather.3.cloned.1.call-update) | async-done | bytes 2097168 | tf_op jit(solution)/shard_map/all_gather | solution.py:72
  100.1 4.1 convert.1
  104.2 60.0 %while.28 = (s32[]{:T(128)}, f32[16,128,256]{2,0,1:T(8,128)S(1)}, s32[]{:T(128)}, s32[96]{0:T(128)S(1)}, bf16[96,128,128]{2,1,0:T(8,128)(2,1)}, /*index=5*/s32[9...) while((s32[]{:T(128)}, f32[16,128,256]{2,0,1:T(8,128)S(1)}, ...), condition=%wide.region_1.0_spmd.clone, body=%wide.region_0.1_spmd.clone.sunk | while | flops 1814039296 | bytes 26219704 | solution.py:50
  104.9 5.0 %gather_fusion = f32[32,128,256]{2,1,0:T(8,128)} fusion(f32[32,128,256]{2,1,0:T(8,128)} %get-tuple-element.535, s32[1024]{0:T(1024)S(1)} %pad_clamp_fusion.4), kind=kCustom, calls=%fused_computation.clone.clone.1 | custom fusion | bytes 8388736 | tf_op jit(solution)/shard_map/while/body/eval_jaxpr/jit(_take)/gather | solution.py:29
  109.9 7.1 %fusion.81 = f32[32,128,256]{2,1,0:T(8,128)} fusion(f32[32,128,256]{2,1,0:T(8,128)} %gather_fusion, pred[32]{0:T(512)(128)(4,1)S(1)} %get-tuple-element.495, bf16[96,128,128]{2,1,0:T(8,128)(2,1)} %get-tuple-element.533, s32[]{:T(128)S(6)} %select_n.98), kind=kOutput, calls=%fused_computation.8.clone.1 | convolution fusion | flops 1611661312 | bytes 9437220 | tf_op jit(solution)/shard_map/while/body/eval_jaxpr/gij,gjw->giw/dot_general | solution.py:31
  117.1 7.1 %select_add_fusion.4 = f32[16,128,256]{2,0,1:T(8,128)S(1)} fusion(f32[16,128,256]{2,0,1:T(8,128)S(1)} %get-tuple-element.519, f32[32,128,256]{2,1,0:T(8,128)} %fusion.81, pred[]{:T(512)S(6)} %compare.6, s32[32]{0:T(128)S(1)} %dynamic_slice.61, pred[32]{0:T(512)(128)(4,1)S(1)} %get-tuple-element.496), kind=kOutput, calls=%fused_computation.10.clone.1 | convolution fusion | flops 202376704 | bytes 8388769 | tf_op jit(solution)/shard_map/while/body/eval_jaxpr/gn,giw->niw/dot_general | solution.py:45
  124.9 5.0 %gather_fusion = f32[32,128,256]{2,1,0:T(8,128)} fusion(f32[32,128,256]{2,1,0:T(8,128)} %get-tuple-element.535, s32[1024]{0:T(1024)S(1)} %pad_clamp_fusion.4), kind=kCustom, calls=%fused_computation.clone.clone.1 | custom fusion | bytes 8388736 | tf_op jit(solution)/shard_map/while/body/eval_jaxpr/jit(_take)/gather | solution.py:29
  129.9 7.1 %fusion.81 = f32[32,128,256]{2,1,0:T(8,128)} fusion(f32[32,128,256]{2,1,0:T(8,128)} %gather_fusion, pred[32]{0:T(512)(128)(4,1)S(1)} %get-tuple-element.495, bf16[96,128,128]{2,1,0:T(8,128)(2,1)} %get-tuple-element.533, s32[]{:T(128)S(6)} %select_n.98), kind=kOutput, calls=%fused_computation.8.clone.1 | convolution fusion | flops 1611661312 | bytes 9437220 | tf_op jit(solution)/shard_map/while/body/eval_jaxpr/gij,gjw->giw/dot_general | solution.py:31
  137.1 7.1 %select_add_fusion.4 = f32[16,128,256]{2,0,1:T(8,128)S(1)} fusion(f32[16,128,256]{2,0,1:T(8,128)S(1)} %get-tuple-element.519, f32[32,128,256]{2,1,0:T(8,128)} %fusion.81, pred[]{:T(512)S(6)} %compare.6, s32[32]{0:T(128)S(1)} %dynamic_slice.61, pred[32]{0:T(512)(128)(4,1)S(1)} %get-tuple-element.496), kind=kOutput, calls=%fused_computation.10.clone.1 | convolution fusion | flops 202376704 | bytes 8388769 | tf_op jit(solution)/shard_map/while/body/eval_jaxpr/gn,giw->niw/dot_general | solution.py:45
  144.9 5.0 %gather_fusion = f32[32,128,256]{2,1,0:T(8,128)} fusion(f32[32,128,256]{2,1,0:T(8,128)} %get-tuple-element.535, s32[1024]{0:T(1024)S(1)} %pad_clamp_fusion.4), kind=kCustom, calls=%fused_computation.clone.clone.1 | custom fusion | bytes 8388736 | tf_op jit(solution)/shard_map/while/body/eval_jaxpr/jit(_take)/gather | solution.py:29
  149.9 7.1 %fusion.81 = f32[32,128,256]{2,1,0:T(8,128)} fusion(f32[32,128,256]{2,1,0:T(8,128)} %gather_fusion, pred[32]{0:T(512)(128)(4,1)S(1)} %get-tuple-element.495, bf16[96,128,128]{2,1,0:T(8,128)(2,1)} %get-tuple-element.533, s32[]{:T(128)S(6)} %select_n.98), kind=kOutput, calls=%fused_computation.8.clone.1 | convolution fusion | flops 1611661312 | bytes 9437220 | tf_op jit(solution)/shard_map/while/body/eval_jaxpr/gij,gjw->giw/dot_general | solution.py:31
  157.1 7.1 %select_add_fusion.4 = f32[16,128,256]{2,0,1:T(8,128)S(1)} fusion(f32[16,128,256]{2,0,1:T(8,128)S(1)} %get-tuple-element.519, f32[32,128,256]{2,1,0:T(8,128)} %fusion.81, pred[]{:T(512)S(6)} %compare.6, s32[32]{0:T(128)S(1)} %dynamic_slice.61, pred[32]{0:T(512)(128)(4,1)S(1)} %get-tuple-element.496), kind=kOutput, calls=%fused_computation.10.clone.1 | convolution fusion | flops 202376704 | bytes 8388769 | tf_op jit(solution)/shard_map/while/body/eval_jaxpr/gn,giw->niw/dot_general | solution.py:45
  164.3 1.3 copy.13
  165.8 63.3 %reduce-scatter.3.cloned.1.call-done = bf16[128,256]{1,0:T(8,128)(2,1)} async-done(((bf16[2048,256]{1,0:T(8,128)(2,1)}), bf16[128,256]{1,0:T(8,128)(2,1)}) %reduce-scatter.3.cloned.1.call-update) | async-done | bytes 65552 | tf_op jit(solution)/shard_map/reduce_scatter | solution.py:79
  229.1 1.1 multiply_reduce_fusion.1
  231.2 86.4 %all-gather.5.cloned.1.call-done = bf16[4096,256]{1,0:T(8,128)(2,1)} async-done(((bf16[128,256]{1,0:T(8,128)(2,1)}), bf16[4096,256]{1,0:T(8,128)(2,1)}) %all-gather.5.cloned.1.call-update) | async-done | bytes 2097168 | tf_op jit(solution)/shard_map/all_gather | solution.py:86
  317.6 46.1 %while.29 = (s32[]{:T(128)}, f32[16,128,256]{2,0,1:T(8,128)}, s32[]{:T(128)}, s32[96]{0:T(128)S(1)}, bf16[96,128,128]{2,1,0:T(8,128)(2,1)}, /*index=5*/s32[96]{0...) while((s32[]{:T(128)}, f32[16,128,256]{2,0,1:T(8,128)}, ...), condition=%wide.region_5.6_spmd.clone, body=%wide.region_4.5_spmd.clone.sunk | while | flops 471862016 | bytes 19928248 | solution.py:50
  318.3 2.3 gather_fusion.1
  320.6 4.0 fusion.86
  324.6 7.9 %select_add_fusion.5 = f32[16,128,256]{2,0,1:T(8,128)} fusion(f32[16,128,256]{2,0,1:T(8,128)} %get-tuple-element.552, f32[32,128,256]{2,1,0:T(8,128)} %fusion.86, pred[]{:T(512)S(6)} %compare.7, s32[32]{0:T(128)S(1)} %dynamic_slice.63, pred[32]{0:T(512)(128)(4,1)S(1)} %get-tuple-element.506), kind=kOutput, calls=%fused_computation.33.clone.1 | convolution fusion | flops 202376704 | bytes 8388769 | tf_op jit(solution)/shard_map/while/body/eval_jaxpr/gn,giw->niw/dot_general | solution.py:45
  333.2 2.3 gather_fusion.1
  335.5 4.0 fusion.86
  339.5 8.5 %select_add_fusion.5 = f32[16,128,256]{2,0,1:T(8,128)} fusion(f32[16,128,256]{2,0,1:T(8,128)} %get-tuple-element.552, f32[32,128,256]{2,1,0:T(8,128)} %fusion.86, pred[]{:T(512)S(6)} %compare.7, s32[32]{0:T(128)S(1)} %dynamic_slice.63, pred[32]{0:T(512)(128)(4,1)S(1)} %get-tuple-element.506), kind=kOutput, calls=%fused_computation.33.clone.1 | convolution fusion | flops 202376704 | bytes 8388769 | tf_op jit(solution)/shard_map/while/body/eval_jaxpr/gn,giw->niw/dot_general | solution.py:45
  348.8 2.3 gather_fusion.1
  351.1 4.0 fusion.86
  355.1 8.5 %select_add_fusion.5 = f32[16,128,256]{2,0,1:T(8,128)} fusion(f32[16,128,256]{2,0,1:T(8,128)} %get-tuple-element.552, f32[32,128,256]{2,1,0:T(8,128)} %fusion.86, pred[]{:T(512)S(6)} %compare.7, s32[32]{0:T(128)S(1)} %dynamic_slice.63, pred[32]{0:T(512)(128)(4,1)S(1)} %get-tuple-element.506), kind=kOutput, calls=%fused_computation.33.clone.1 | convolution fusion | flops 202376704 | bytes 8388769 | tf_op jit(solution)/shard_map/while/body/eval_jaxpr/gn,giw->niw/dot_general | solution.py:45
  363.7 1.7 convert_element_type.41
  365.4 1.3 copy.14
  366.8 63.4 %reduce-scatter.5.cloned.1.call-done = bf16[128,256]{1,0:T(8,128)(2,1)} async-done(((bf16[2048,256]{1,0:T(8,128)(2,1)}), bf16[128,256]{1,0:T(8,128)(2,1)}) %reduce-scatter.5.cloned.1.call-update) | async-done | bytes 65552 | tf_op jit(solution)/shard_map/reduce_scatter | solution.py:91
  430.2 1.1 fusion.56
  431.6 0.7 multiply_convert_fusion
  (54 shorter events, 6.4 us)
Async XLA Ops:
  6.5 424.8 %copy-start = (bf16[256,256]{1,0:T(8,128)(2,1)S(1)}, bf16[256,256]{1,0:T(8,128)(2,1)}, u32[]{:S(2)}) copy-start(bf16[256,256]{1,0:T(8,128)(2,1)} %param.25) | copy-start | bytes 393220
  6.5 93.5 %all-gather.3.cloned.1.call-start = ((), (), s32[]{:S(2)}) async-start(), calls=%async_computation.2 | async-start | bytes 2162688 | tf_op jit(solution)/shard_map/all_gather | solution.py:72
  8.2 220.8 %reduce-scatter.3.cloned.1.call-start = ((), (), s32[]{:S(2)}) async-start(), calls=%async_computation.3 | async-start | bytes 1114112 | tf_op jit(solution)/shard_map/reduce_scatter | solution.py:79
  100.1 4.1 copy-start.2
  100.1 4.1 copy-start.9
  164.3 1.5 copy-start.8
  164.3 64.8 %copy-start.3 = (bf16[128,128]{1,0:T(8,128)(2,1)S(1)}, bf16[128,128]{1,0:T(8,128)(2,1)}, u32[]{:S(2)}) copy-start(bf16[128,128]{1,0:T(8,128)(2,1)} %param.16) | copy-start | bytes 98308
  164.3 64.8 %copy-start.6 = (bf16[128,256]{1,0:T(8,128)(2,1)S(1)}, bf16[128,256]{1,0:T(8,128)(2,1)}, u32[]{:S(2)}) copy-start(bf16[128,256]{1,0:T(8,128)(2,1)} %param.22) | copy-start | bytes 196612
  164.3 64.8 %copy-start.7 = (f32[256]{0:T(256)S(1)}, f32[256]{0:T(256)}, u32[]{:S(2)}) copy-start(f32[256]{0:T(256)} %param.24) | copy-start | bytes 3076
  165.7 151.9 %all-gather.5.cloned.1.call-start = ((), (), s32[]{:S(2)}) async-start(), calls=%async_computation.4 | async-start | bytes 2162688 | tf_op jit(solution)/shard_map/all_gather | solution.py:86
  230.9 199.3 %reduce-scatter.5.cloned.1.call-start = ((), (), s32[]{:S(2)}) async-start(), calls=%async_computation.5 | async-start | bytes 1114112 | tf_op jit(solution)/shard_map/reduce_scatter | solution.py:91
  365.4 64.8 %copy-start.5 = (bf16[256,256]{1,0:T(8,128)(2,1)S(1)}, bf16[256,256]{1,0:T(8,128)(2,1)}, u32[]{:S(2)}) copy-start(bf16[256,256]{1,0:T(8,128)(2,1)} %param.26) | copy-start | bytes 393220
  365.4 65.9 %copy-start.1 = (bf16[128,256]{1,0:T(8,128)(2,1)S(1)}, bf16[128,256]{1,0:T(8,128)(2,1)}, u32[]{:S(2)}) copy-start(bf16[128,256]{1,0:T(8,128)(2,1)} %multiply_convert_fusion.1) | copy-start | bytes 196612
  365.4 65.9 %copy-start.4 = (f32[256]{0:T(256)S(1)}, f32[256]{0:T(256)}, u32[]{:S(2)}) copy-start(f32[256]{0:T(256)} %param.27) | copy-start | bytes 3076
Sparse Core Ops, SparseCore 0:
  10.5 89.4 all-gather.2
  165.8 63.2 reduce-scatter.2
  232.7 84.7 all-gather.4
  366.9 63.2 reduce-scatter.4
where the time goes:
time: 441 us; the launch traced here: 439 us
  waiting for transfers between devices  305 us (69%)
  matrix products  83.5 us (19%)
  local copies, waits for them, and re-layouts  24.9 us (6%)
  between operations  13.3 us (3%)
  other arithmetic  11.8 us (3%)
    all_gather x1, waiting for transfers between devices, shards(): lax.all_gather(projected.astype(jnp.bfloat16), 'row', axis=0, tiled=True)  91.8 us
    all_gather x1, waiting for transfers between devices, shards(): hidden_rows = lax.all_gather(hidden, 'row', axis=0, tiled=True)  86.4 us
    reduce_scatter x1, waiting for transfers between devices, shards(): lax.psum_scatter(partial_two.astype(jnp.bfloat16), 'col', scatter_dimensi...  63.4 us
    reduce_scatter x1, waiting for transfers between devices, shards(): lax.psum_scatter(partial_value.astype(jnp.bfloat16), 'col', scatter_dimen...  63.3 us
    dot_general x6, matrix products, add_group(): jnp.einsum('gn,giw->niw', onehot, products, precision=lax.Precision.HIGHEST)  46.1 us
    gather x6, local copies, waits for them, and re-layouts, add_group(): picked = jnp.take(source_tiles, src_block, axis=0)  21.8 us
    dot_general x3, matrix products, add_group(): jnp.einsum('gij,gjw->giw', tile_block.astype(jnp.float32), picked, precis...  21.3 us
    dot_general x3, matrix products, add_group(): jnp.einsum('gij,gjw->giw', tile_block, picked, preferred_element_type=jnp...  11.9 us
  transfers between devices with their start and end apart: 4, of which 4 were waited for; matrix products, arithmetic and copies ran while one was open for 0% of the time, Pallas kernels for 0%

commit v1 on v0

v1 whole, which is shorter than its diff:
```python
import jax
import jax.numpy as jnp
from jax import lax
from jax.experimental import pallas as pl
from jax.experimental.pallas import tpu as pltpu
from jax.sharding import PartitionSpec as P

NY, NZ = 8, 4
NX, NL, NC = 4, 2, 2
B = 128
SLOTS = 96
NDEST = NX * NL * NC
BF, F32, I32 = jnp.bfloat16, jnp.float32, jnp.int32
MESH = pl.DeviceIdType.MESH
X_ORDER = (2, 1, 3, 0)
LAG = 2


def mod(value, size):
    return lax.rem(value + size, jnp.int32(size))


def relu_norm(pre):
    positive = jnp.maximum(pre, 0.0)
    mean_square = jnp.mean(positive * positive, axis=-1, keepdims=True)
    return (positive * lax.rsqrt(mean_square + 1e-05)).astype(BF)


def mm(a, b):
    return jnp.dot(a, b, preferred_element_type=F32)


def mm_split(a, b):
    high = a.astype(BF)
    low = (a - high.astype(F32)).astype(BF)
    return mm(high, b) + mm(low, b)


def kernel(
    features, tiles, dest, src, live, degrees, w_self1, w_neigh1, bias1, w_self2, w_neigh2, bias2,
    out,
    xg, adj, tile_in, tile_f, tile_b, acc, send1, recv1, send2, recv2, tab_v, tab_s,
    ws1, wn1, ws2, wn2, divisor, self_part,
    load_sem, zs, zr, ys, yr, s1s, s1r, s2s, s2r,
):
    row, col = lax.axis_index("row"), lax.axis_index("col")
    y, z = lax.div(row, jnp.int32(NZ)), lax.rem(row, jnp.int32(NZ))
    x = lax.div(col, jnp.int32(NL * NC))
    zl = lax.rem(lax.div(col, jnp.int32(NC)), jnp.int32(NL))
    core = lax.rem(col, jnp.int32(NC))

    def at_y(dy):
        return (mod(y + dy, NY) * NZ + z, col)

    def at_z(dz):
        return (y * NZ + mod(z + dz, NZ), col)

    def at_xl(dx, dl):
        return (row, (mod(x + dx, NX) * NL + mod(zl + dl, NL)) * NC + core)

    other_core = (row, col + 1 - 2 * core)

    load_features = pltpu.make_async_copy(features, xg.at[0, y, z], load_sem.at[0])
    load_tiles = pltpu.make_async_copy(tiles, tile_in, load_sem.at[1])
    weight_loads = [
        pltpu.make_async_copy(a, b, load_sem.at[3 + i])
        for i, (a, b) in enumerate(((w_self1, ws1), (w_neigh1, wn1), (w_self2, ws2), (w_neigh2, wn2)))
    ]
    load_features.start()
    load_tiles.start()
    for load in weight_loads:
        load.start()

    barrier = pltpu.get_barrier_semaphore()
    partners = [at_y(1), at_y(-1)]
    partners += [at_z(dz) for dz in range(1, NZ)]
    partners += [at_xl(dx, dl) for dx in range(NX) for dl in range(NL) if dx or dl]
    partners += [other_core]
    for partner in partners:
        pl.semaphore_signal(barrier, inc=1, device_id=partner, device_id_type=MESH)
    pl.semaphore_wait(barrier, len(partners))

    def remote(a, b, ss, rs, device):
        return pltpu.make_async_remote_copy(
            src_ref=a, dst_ref=b, send_sem=ss, recv_sem=rs, device_id=device, device_id_type=MESH
        )

    started = []

    def send(a, b, ss, rs, device):
        copy = remote(a, b, ss, rs, device)
        copy.start()
        started.append(copy)

    def z_send(p):
        for dz in (1, 3, 2):
            ref = xg.at[p, y, z]
            send(ref, ref, zs.at[p, dz - 1], zr.at[p, dz - 1], at_z(dz))

    def piece(p, k, way, dz):
        return xg.at[p, mod(y - k if way == 0 else y + k, NY), mod(z - dz, NZ)]

    def carries(k, way, dz):
        return k < NY // 2 or (dz < NZ // 2) == (way == 0)

    def forward(p, k, way, dz):
        if k + 1 <= NY // 2 and carries(k + 1, way, dz):
            ref = piece(p, k, way, dz)
            send(ref, ref, ys.at[p, way, k, dz], yr.at[p, way, k, dz], at_y(1 if way == 0 else -1))

    def wait_piece(p, k, way, dz):
        ref = piece(p, k, way, dz)
        remote(ref, ref, ys.at[p, way, k - 1, dz], yr.at[p, way, k - 1, dz], at_y(-1 if way == 0 else 1)).wait_recv()

    def step(p, k):
        for dz in (0, 1, 3, 2):
            if k == 0:
                if dz:
                    ref = xg.at[p, y, mod(z - dz, NZ)]
                    remote(ref, ref, zs.at[p, dz - 1], zr.at[p, dz - 1], at_z(-dz)).wait_recv()
                for way in (0, 1):
                    forward(p, 0, way, dz)
            else:
                for way in (0, 1):
                    if carries(k, way, dz):
                        wait_piece(p, k, way, dz)
                        forward(p, k, way, dz)

    def bundles(k):
        if k == 0:
            return [y]
        if k == NY // 2:
            return [mod(y + k, NY)]
        return [mod(y - k, NY), mod(y + k, NY)]

    def product(p, k, block_x):
        total = None
        for b in bundles(k):
            lhs = adj[b, pl.ds(block_x * (NL * NC), NL * NC)].reshape(NL * NC * B, NZ * B)
            part = mm(lhs, xg[p, b].reshape(NZ * B, B))
            total = part if total is None else total + part
        return total.reshape(NL * NC, B, B)

    def compute(p, k):
        @pl.loop(0, NX)
        def _(block_x):
            rows = pl.ds(block_x * (NL * NC), NL * NC)
            value = product(p, k, block_x)
            if k:
                value = value + acc[p, rows]
            acc[p, rows] = value

    def dest_block(dx, dl, c):
        return (mod(x + dx, NX) * NL + mod(zl + dl, NL)) * NC + c

    def finish_and_exchange(p):
        for i, dx in enumerate(X_ORDER):
            block_x = mod(x + dx, NX)
            rows = pl.ds(block_x * (NL * NC), NL * NC)
            acc[p, rows] = product(p, NY // 2, block_x) + acc[p, rows]
            for dl in range(NL):
                send1[p, i, dl] = acc[p, dest_block(dx, dl, 1 - core)].astype(BF)
            send(send1.at[p, i], recv1.at[p, i], s1s.at[p, i], s1r.at[p, i], other_core)

    def scatter(p):
        for i, dx in enumerate(X_ORDER):
            remote(send1.at[p, i], recv1.at[p, i], s1s.at[p, i], s1r.at[p, i], other_core).wait_recv()
            for dl in (1, 0):
                d = dest_block(dx, dl, core)
                value = acc[p, d] + recv1[p, i, dl].astype(F32)
                if dx or dl:
                    j = dx * NL + dl - 1
                    send2[p, j] = value.astype(BF)
                    send(send2.at[p, j], recv2.at[p, j], s2s.at[p, j], s2r.at[p, j], at_xl(dx, dl))
                else:
                    acc[p, d] = value

    def collect(p):
        total = acc[p, dest_block(0, 0, core)]
        for j in range(NX * NL - 1):
            dx, dl = divmod(j + 1, NL)
            remote(send2.at[p, j], recv2.at[p, j], s2s.at[p, j], s2r.at[p, j], at_xl(-dx, -dl)).wait_recv()
            total = total + recv2[p, j].astype(F32)
        return total / divisor[...]

    load_features.wait()
    z_send(0)
    for way in (0, 1):
        forward(0, 0, way, 0)

    lane = lax.broadcasted_iota(I32, (1, B), 1)
    tab_v[...] = jnp.zeros_like(tab_v)
    tab_v[0:1, 0:SLOTS] = dest[...]
    tab_v[1:2, 0:SLOTS] = src[...]
    place = jnp.where(lane < live[0], tab_v[1:2, :] * NDEST + tab_v[0:1, :], -1)
    place_j = jnp.broadcast_to(place, (B, B)).T
    slot_j = lax.broadcasted_iota(I32, (B, B), 0)
    lanes = lax.broadcasted_iota(I32, (B, B), 1)

    def lowest(mask):
        return jnp.min(jnp.where(mask, slot_j, SLOTS), axis=0, keepdims=True)

    for i in range(NY * NZ * NDEST // B):
        tab_v[i : i + 1, :] = lowest(place_j == lanes + i * B)
    tab_v[4:5, :] = lowest((place_j == place) & (slot_j > lanes) & (place >= 0))
    load_table = pltpu.make_async_copy(tab_v, tab_s, load_sem.at[2])
    load_table.start()
    divisor[...] = jnp.broadcast_to(degrees[...].astype(F32), (B, B)).T
    load_table.wait()
    load_tiles.wait()

    def slot_at(i, j):
        return lax.clamp(jnp.int32(0), tab_s[i, j], jnp.int32(SLOTS))

    tile_f[SLOTS] = jnp.zeros((B, B), F32)
    tile_b[SLOTS] = jnp.zeros((B, B), BF)

    @pl.loop(0, SLOTS)
    def _(i):
        slot = SLOTS - 1 - i
        value = tile_in[slot].astype(F32) + tile_f[slot_at(4, slot)]
        tile_f[slot] = value
        tile_b[slot] = value.astype(BF)

    def build(k):
        for b in bundles(k):
            @pl.loop(0, NDEST)
            def _(d):
                for zz in range(NZ):
                    entry = b * (NZ * NDEST) + zz * NDEST + d
                    slot = slot_at(lax.div(entry, jnp.int32(B)), lax.rem(entry, jnp.int32(B)))
                    adj[b, d, :, zz * B : (zz + 1) * B] = tile_b[slot]

    for k in range(NY // 2):
        if k == 0:
            for dz in (1, 3, 2):
                ref = xg.at[0, y, mod(z - dz, NZ)]
                remote(ref, ref, zs.at[0, dz - 1], zr.at[0, dz - 1], at_z(-dz)).wait_recv()
                for way in (0, 1):
                    forward(0, 0, way, dz)
        else:
            step(0, k)
        build(k)
        compute(0, k)
    build(NY // 2)
    for load in weight_loads:
        load.wait()
    own = xg[0, y, z]
    self_part[...] = mm(own, ws1[...]) + bias1[...]
    step(0, NY // 2)
    finish_and_exchange(0)
    scatter(0)
    first = collect(0)
    hidden = relu_norm(self_part[...] + mm_split(first, wn1[...]))
    xg[1, y, z] = hidden[:, :B]
    xg[2, y, z] = hidden[:, B:]

    z_send(1)
    z_send(2)
    last = NY // 2
    for t in range(last + LAG + 1):
        if t <= last:
            step(1, t)
        if 0 <= t - LAG <= last:
            step(2, t - LAG)
        if t == 0:
            self_part[...] = mm(hidden, ws2[...]) + bias2[...]
        if t < last:
            compute(1, t)
        if t == last:
            finish_and_exchange(1)
        if t == last + 1:
            scatter(1)
        if t == last + 2:
            self_part[...] += mm_split(collect(1), wn2[0:B, :])
        if 0 <= t - LAG < last:
            compute(2, t - LAG)
    finish_and_exchange(2)
    scatter(2)
    out[...] = relu_norm(self_part[...] + mm_split(collect(2), wn2[B:, :]))
    for copy in started:
        copy.wait_send()


def shards(
    features, adj_tiles, tile_dest, tile_src, live_tiles, degrees,
    self_one, neigh_one, bias_one, self_two, neigh_two, bias_two,
):
    hid = self_one.shape[1]
    any_spec = pl.BlockSpec(memory_space=pl.ANY)
    vmem_spec = pl.BlockSpec(memory_space=pltpu.VMEM)
    smem_spec = pl.BlockSpec(memory_space=pltpu.SMEM)
    sem = pltpu.SemaphoreType.DMA
    return pl.pallas_call(
        kernel,
        out_shape=jax.ShapeDtypeStruct((B, hid), BF),
        in_specs=[
            any_spec, any_spec, vmem_spec, vmem_spec, smem_spec, vmem_spec,
            any_spec, any_spec, vmem_spec, any_spec, any_spec, vmem_spec,
        ],
        out_specs=vmem_spec,
        scratch_shapes=[
            pltpu.VMEM((3, NY, NZ, B, B), BF),
            pltpu.VMEM((NY, NDEST, B, NZ * B), BF),
            pltpu.VMEM((SLOTS, B, B), BF),
            pltpu.VMEM((SLOTS + 1, B, B), F32),
            pltpu.VMEM((SLOTS + 1, B, B), BF),
            pltpu.VMEM((3, NDEST, B, B), F32),
            pltpu.VMEM((3, NX, NL, B, B), BF),
            pltpu.VMEM((3, NX, NL, B, B), BF),
            pltpu.VMEM((3, NX * NL - 1, B, B), BF),
            pltpu.VMEM((3, NX * NL - 1, B, B), BF),
            pltpu.VMEM((8, B), I32),
            pltpu.SMEM((8, B), I32),
            pltpu.VMEM((B, hid), BF),
            pltpu.VMEM((B, hid), BF),
            pltpu.VMEM((hid, hid), BF),
            pltpu.VMEM((hid, hid), BF),
            pltpu.VMEM((B, B), F32),
            pltpu.VMEM((B, hid), F32),
            sem((7,)),
            sem((3, NZ - 1)),
            sem((3, NZ - 1)),
            sem((3, 2, NY // 2, NZ)),
            sem((3, 2, NY // 2, NZ)),
            sem((3, NX)),
            sem((3, NX)),
            sem((3, NX * NL - 1)),
            sem((3, NX * NL - 1)),
        ],
        compiler_params=pltpu.CompilerParams(
            collective_id=0, has_side_effects=True, vmem_limit_bytes=56 * 1024 * 1024
        ),
    )(
        features, adj_tiles, tile_dest[None], tile_src[None], live_tiles, degrees[None],
        self_one, neigh_one, bias_one[None], self_two, neigh_two, bias_two[None],
    )


def solution(mesh):
    rows = P(("row", "col"))
    in_specs = (rows,) * 6 + (P(),) * 6
    return jax.shard_map(shards, mesh=mesh, in_specs=in_specs, out_specs=rows, check_vma=False)
```

time: 441 us -> 93.3 us (0.21)
  waiting for transfers between devices: 305 us -> 0 us
  Pallas kernels: 0 us -> 91 us
  matrix products: 83.5 us -> 0 us
  local copies, waits for them, and re-layouts: 24.9 us -> 1.47 us
  between operations: 13.3 us -> 0.66 us
  other arithmetic: 11.8 us -> 0 us
    all_gather x2 -> x0, waiting for transfers between devices: 178 us -> none  [the longest x1 91.8 us: shards(): lax.all_gather(projected.astype(jnp.bfloat16), 'row', axis=0, tiled=True)]
    reduce_scatter x2 -> x0, waiting for transfers between devices: 127 us -> none  [the longest x1 63.4 us: shards(): lax.psum_scatter(partial_two.astype(jnp.bfloat16), 'col', scatter_dimensi...]
    pallas_call x0 -> x1, Pallas kernels: none -> 91 us  [shards(): pl.pallas_call(kernel, out_shape=jax.ShapeDtypeStruct((B, hid), BF), in_s...]
    dot_general x16 -> x0, matrix products: 83.5 us -> none  [the longest x6 46.1 us: add_group(): jnp.einsum('gn,giw->niw', onehot, products, precision=lax.Precision.HIGHEST)]
    gather x6 -> x0, local copies, waits for them, and re-layouts: 21.8 us -> none  [add_group(): picked = jnp.take(source_tiles, src_block, axis=0)]
  transfers between devices with their start and end apart: 4 -> 0, of which waited for: 4 -> 0; matrix products, arithmetic and copies ran while one was open for 0% -> 0% of each run, Pallas kernels for 0% -> 0%
where the time goes in v1:
time: 93.3 us; the launch traced here: 93.2 us
  Pallas kernels  91 us (98%)
  local copies, waits for them, and re-layouts  1.47 us (2%)
    pallas_call x1, Pallas kernels, shards(): pl.pallas_call(kernel, out_shape=jax.ShapeDtypeStruct((B, hid), BF), in_s...  91 us

profile of v1, /device:TPU:1, one launch (start us, length us, event | category | flops | bytes accessed | tf_op | source)
XLA Modules:
  0.0 93.2 jit_solution(7336895733977414696)
XLA Ops:
  0.7 91.0 %shard_map.118 = bf16[128,256]{1,0:T(8,128)(2,1)} custom-call(bf16[128,128]{1,0:T(8,128)(2,1)} %features.1, bf16[96,128,128]{2,1,0:T(8,128)(2,1)} %tiles.1, s32[1,96]{1,0:T(1,128)} %bitcast.7, s32[1,96]{1,0:T(1,128)} %bitcast.8, s32[1]{0:T(128)S(6)} %copy.14.live, s32[1,128]{1,0:T(1,128)} %bitcast.9, bf16[128,256]{1,0:T(8,128)(2,1)} %w_self1.1, ...), custom_call_target="tpu_custom_call" | custom-call | tf_op jit(solution)/shard_map/pallas_call | solution.py:294
  91.7 1.5 %copy.15 = bf16[128,256]{1,0:T(8,128)(2,1)} copy(bf16[128,256]{1,0:T(8,128)(2,1)} %shard_map.118) | data formatting | bytes 131072
